TPU v7x, 32 devices: a whole 2x2x4 slice. The times are simulated.
32 devices in a mesh: blk: 4 (over z), src: 2 (over x), layer: 4 (over y, core).
Axes of the slice: x: 2, y: 2, z: 4, core: 2. Of those that a mesh axis runs over, the one named last changes fastest.
Arguments:
- resident_act: bfloat16 [4, 2048, 4096], P('layer', 'blk'), may hold values from -6 to 6
- resident_grad: bfloat16 [4, 2048, 4096], P('layer', 'blk'), may hold values from -6 to 6
- source_act: bfloat16 [4, 128, 4096], P('layer', ('blk', 'src')), may hold values from -6 to 6
- source_grad: bfloat16 [4, 128, 4096], P('layer', ('blk', 'src')), may hold values from -6 to 6
- probes: bfloat16 [128, 256], P(('blk', 'src')), may hold values from -6 to 6
Outputs:
- kernel_product: float32 [2048, 256], P(('blk', 'layer'))
All inputs are finite; a program needn't handle non-finite values.
Results may differ from a plain program's by a relative error of at most 0.0029.
Values may be sent and summed in bfloat16 or wider, within the bound.
A program may use at most 64 MiB of HBM per device.

v0:
```python
import jax
import jax.numpy as jnp
from jax import lax
from jax.sharding import PartitionSpec as P

LAYERS = 4


def shifted(shard, axis, by):
    length = lax.axis_size(axis)
    return lax.ppermute(shard, axis, [(i, (i + by) % length) for i in range(length)])


def contract_rows(left, right):
    return lax.dot_general(
        left, right, (((1,), (1,)), ((), ())), preferred_element_type=jnp.float32
    )


def on_device(resident_act, resident_grad, source_act, source_grad, probes):
    width = resident_act.shape[2]
    blocks = lax.axis_size("blk")
    source_total = source_act.shape[1] * blocks * lax.axis_size("src")
    inverse_width = jnp.float32(1.0 / width)

    def accumulate(total, acts, grads, probe_rows):
        act_gram = contract_rows(acts[0], resident_act[0])
        grad_gram = contract_rows(grads[0], resident_grad[0])
        kernel = (act_gram * grad_gram * inverse_width).astype(jnp.bfloat16)
        total = total + lax.dot_general(
            kernel, probe_rows, (((0,), (0,)), ((), ())), preferred_element_type=jnp.float32
        )
        return total

    total = jnp.zeros((resident_act.shape[1], probes.shape[1]), jnp.float32)

    def turn(step, carry):
        acc, acts, grads, probe_rows = carry
        acc = accumulate(acc, acts, grads, probe_rows)
        acts, grads, probe_rows = shifted((acts, grads, probe_rows), "blk", 1)
        return (acc, acts, grads, probe_rows)

    total, acts, grads, probe_rows = lax.fori_loop(
        0, blocks - 1, turn, (total, source_act, source_grad, probes)
    )
    total = accumulate(total, acts, grads, probe_rows)
    groups = lax.axis_size("src")
    layer_groups = lax.axis_size("layer")
    share = total.shape[0] // (groups * layer_groups)
    reordered = total.reshape(layer_groups, groups, share, total.shape[1])
    reordered = jnp.transpose(reordered, (1, 0, 2, 3)).reshape(total.shape)
    partial_rows = lax.psum_scatter(reordered, ("src", "layer"), scatter_dimension=0, tiled=True)
    result = lax.all_gather(partial_rows, "src", axis=0, tiled=True)
    return result * jnp.float32((LAYERS * source_total) ** (-0.5))


def solution(mesh):
    in_specs = (
        P("layer", "blk", None),
        P("layer", "blk", None),
        P("layer", ("blk", "src"), None),
        P("layer", ("blk", "src"), None),
        P(("blk", "src"), None),
    )
    out_specs = P(("blk", "layer"), None)
    return jax.shard_map(
        on_device, mesh=mesh, in_specs=in_specs, out_specs=out_specs, check_vma=False
    )
```

profile of v0, /device:TPU:0, one launch (start us, length us, event | category | flops | bytes accessed | tf_op | source)
XLA Modules:
  0.0 99.2 jit_solution(2952006755131350569)
XLA Ops:
  6.5 0.7 copy.27
  7.2 0.9 copy.25
  8.1 0.9 copy.26
  9.0 35.1 %while.17 = (s32[]{:T(128)}, f32[512,256]{1,0:T(8,128)S(1)}, bf16[1,16,4096]{2,1,0:T(8,128)(2,1)S(1)}, bf16[1,16,4096]{2,1,0:T(8,128)(2,1)S(1)}, bf16[16,256]{1,...) while((s32[]{:T(128)}, f32[512,256]{1,0:T(8,128)S(1)}, ...), condition=%wide.region_1.0_spmd.clone, body=%wide.region_0.0_spmd.clone.sunk | while | flops 138698752 | bytes 11395295 | solution.py:43
  9.0 3.0 %collective-permute-start.2 = (bf16[16,256]{1,0:T(8,128)(2,1)S(1)}, bf16[16,256]{1,0:T(8,128)(2,1)S(1)}, u32[]{:S(2)}, u32[]{:S(2)}) collective-permute-start(bf16[16,256]{1,0:T(8,128)(2,1)S(1)} %copy.16), channel_id=1, source_target_pairs={{0,8},{8,16},{16,24},{24,0},{1,9},{9,17},{17,25},{25,1},{2,10},{10... | collective-permute-start | bytes 24584 | tf_op jit(solution)/shard_map/while/body/eval_jaxpr/ppermute | solution.py:11
  12.1 1.6 %collective-permute-start = (bf16[1,16,4096]{2,1,0:T(8,128)(2,1)S(1)}, bf16[1,16,4096]{2,1,0:T(8,128)(2,1)S(1)}, u32[]{:S(2)}, u32[]{:S(2)}) collective-permute-start(bf16[1,16,4096]{2,1,0:T(8,128)(2,1)S(1)} %copy.14), channel_id=1, source_target_pairs={{0,8},{8,16},{16,24},{24,0},{1,9},{9,17},{17,25},{25,1},{2,10},{10... | collective-permute-start | bytes 393224 | tf_op jit(solution)/shard_map/while/body/eval_jaxpr/ppermute | solution.py:11
  13.7 1.6 %collective-permute-start.1 = (bf16[1,16,4096]{2,1,0:T(8,128)(2,1)S(1)}, bf16[1,16,4096]{2,1,0:T(8,128)(2,1)S(1)}, u32[]{:S(2)}, u32[]{:S(2)}) collective-permute-start(bf16[1,16,4096]{2,1,0:T(8,128)(2,1)S(1)} %copy.15), channel_id=1, source_target_pairs={{0,8},{8,16},{16,24},{24,0},{1,9},{9,17},{17,25},{25,1},{2,10},{10... | collective-permute-start | bytes 393224 | tf_op jit(solution)/shard_map/while/body/eval_jaxpr/ppermute | solution.py:11
  15.4 3.4 %fusion.53 = f32[16,512]{1,0:T(8,128)S(1)} fusion(bf16[1,512,4096]{2,1,0:T(8,128)(2,1)} %get-tuple-element.154, bf16[1,16,4096]{2,1,0:T(8,128)(2,1)S(1)} %copy.15), kind=kOutput, calls=%fused_computation.clone.1 | convolution fusion | flops 67108864 | bytes 4358144 | tf_op jit(solution)/shard_map/while/body/eval_jaxpr/dot_general | solution.py:15
  18.7 3.8 %convolution_add_fusion.3 = f32[512,256]{1,0:T(8,128)S(1)} fusion(bf16[16,256]{1,0:T(8,128)(2,1)S(1)} %copy.16, f32[16,512]{1,0:T(8,128)S(1)} %fusion.53, bf16[1,512,4096]{2,1,0:T(8,128)(2,1)} %get-tuple-element.153, f32[512,256]{1,0:T(8,128)S(1)} %get-tuple-element.140, pred[]{:T(512)S(6)} %compare.3, bf16[1,16,4096]{2,1,0:T(8,128)(2,1)S(1)} %copy.14), kind=kOutput, calls=%fused_computation.4.clone.1 | convolution fusion | flops 71589888 | bytes 5414913 | tf_op jit(solution)/shard_map/while/body/eval_jaxpr/dot_general | solution.py:30
  22.5 0.0 collective-permute-done.2
  22.5 0.0 collective-permute-done
  22.5 0.0 collective-permute-done.1
  22.6 0.1 collective-permute-start.2
  22.7 1.8 %collective-permute-start = (bf16[1,16,4096]{2,1,0:T(8,128)(2,1)S(1)}, bf16[1,16,4096]{2,1,0:T(8,128)(2,1)S(1)}, u32[]{:S(2)}, u32[]{:S(2)}) collective-permute-start(bf16[1,16,4096]{2,1,0:T(8,128)(2,1)S(1)} %copy.14), channel_id=1, source_target_pairs={{0,8},{8,16},{16,24},{24,0},{1,9},{9,17},{17,25},{25,1},{2,10},{10... | collective-permute-start | bytes 393224 | tf_op jit(solution)/shard_map/while/body/eval_jaxpr/ppermute | solution.py:11
  24.5 1.6 %collective-permute-start.1 = (bf16[1,16,4096]{2,1,0:T(8,128)(2,1)S(1)}, bf16[1,16,4096]{2,1,0:T(8,128)(2,1)S(1)}, u32[]{:S(2)}, u32[]{:S(2)}) collective-permute-start(bf16[1,16,4096]{2,1,0:T(8,128)(2,1)S(1)} %copy.15), channel_id=1, source_target_pairs={{0,8},{8,16},{16,24},{24,0},{1,9},{9,17},{17,25},{25,1},{2,10},{10... | collective-permute-start | bytes 393224 | tf_op jit(solution)/shard_map/while/body/eval_jaxpr/ppermute | solution.py:11
  26.1 3.4 %fusion.53 = f32[16,512]{1,0:T(8,128)S(1)} fusion(bf16[1,512,4096]{2,1,0:T(8,128)(2,1)} %get-tuple-element.154, bf16[1,16,4096]{2,1,0:T(8,128)(2,1)S(1)} %copy.15), kind=kOutput, calls=%fused_computation.clone.1 | convolution fusion | flops 67108864 | bytes 4358144 | tf_op jit(solution)/shard_map/while/body/eval_jaxpr/dot_general | solution.py:15
  29.5 3.8 %convolution_add_fusion.3 = f32[512,256]{1,0:T(8,128)S(1)} fusion(bf16[16,256]{1,0:T(8,128)(2,1)S(1)} %copy.16, f32[16,512]{1,0:T(8,128)S(1)} %fusion.53, bf16[1,512,4096]{2,1,0:T(8,128)(2,1)} %get-tuple-element.153, f32[512,256]{1,0:T(8,128)S(1)} %get-tuple-element.140, pred[]{:T(512)S(6)} %compare.3, bf16[1,16,4096]{2,1,0:T(8,128)(2,1)S(1)} %copy.14), kind=kOutput, calls=%fused_computation.4.clone.1 | convolution fusion | flops 71589888 | bytes 5414913 | tf_op jit(solution)/shard_map/while/body/eval_jaxpr/dot_general | solution.py:30
  33.3 0.0 collective-permute-done
  33.4 1.6 %collective-permute-start.2 = (bf16[16,256]{1,0:T(8,128)(2,1)S(1)}, bf16[16,256]{1,0:T(8,128)(2,1)S(1)}, u32[]{:S(2)}, u32[]{:S(2)}) collective-permute-start(bf16[16,256]{1,0:T(8,128)(2,1)S(1)} %copy.16), channel_id=1, source_target_pairs={{0,8},{8,16},{16,24},{24,0},{1,9},{9,17},{17,25},{25,1},{2,10},{10... | collective-permute-start | bytes 24584 | tf_op jit(solution)/shard_map/while/body/eval_jaxpr/ppermute | solution.py:11
  35.0 0.1 collective-permute-start
  35.1 1.8 %collective-permute-start.1 = (bf16[1,16,4096]{2,1,0:T(8,128)(2,1)S(1)}, bf16[1,16,4096]{2,1,0:T(8,128)(2,1)S(1)}, u32[]{:S(2)}, u32[]{:S(2)}) collective-permute-start(bf16[1,16,4096]{2,1,0:T(8,128)(2,1)S(1)} %copy.15), channel_id=1, source_target_pairs={{0,8},{8,16},{16,24},{24,0},{1,9},{9,17},{17,25},{25,1},{2,10},{10... | collective-permute-start | bytes 393224 | tf_op jit(solution)/shard_map/while/body/eval_jaxpr/ppermute | solution.py:11
  36.9 3.4 %fusion.53 = f32[16,512]{1,0:T(8,128)S(1)} fusion(bf16[1,512,4096]{2,1,0:T(8,128)(2,1)} %get-tuple-element.154, bf16[1,16,4096]{2,1,0:T(8,128)(2,1)S(1)} %copy.15), kind=kOutput, calls=%fused_computation.clone.1 | convolution fusion | flops 67108864 | bytes 4358144 | tf_op jit(solution)/shard_map/while/body/eval_jaxpr/dot_general | solution.py:15
  40.3 3.8 %convolution_add_fusion.3 = f32[512,256]{1,0:T(8,128)S(1)} fusion(bf16[16,256]{1,0:T(8,128)(2,1)S(1)} %copy.16, f32[16,512]{1,0:T(8,128)S(1)} %fusion.53, bf16[1,512,4096]{2,1,0:T(8,128)(2,1)} %get-tuple-element.153, f32[512,256]{1,0:T(8,128)S(1)} %get-tuple-element.140, pred[]{:T(512)S(6)} %compare.3, bf16[1,16,4096]{2,1,0:T(8,128)(2,1)S(1)} %copy.14), kind=kOutput, calls=%fused_computation.4.clone.1 | convolution fusion | flops 71589888 | bytes 5414913 | tf_op jit(solution)/shard_map/while/body/eval_jaxpr/dot_general | solution.py:30
  44.1 0.0 collective-permute-done.2
  44.1 0.0 collective-permute-done.1
  44.1 3.4 %fusion.20 = f32[16,512]{1,0:T(8,128)S(1)} fusion(bf16[1,512,4096]{2,1,0:T(8,128)(2,1)} %get-tuple-element.158, bf16[1,16,4096]{2,1,0:T(8,128)(2,1)S(1)} %get-tuple-element.47), kind=kOutput, calls=%fused_computation.12 | convolution fusion | flops 67108864 | bytes 4358144 | tf_op jit(solution)/shard_map/dot_general | solution.py:15
  47.5 3.7 %convolution_add_fusion.1 = f32[512,256]{1,0:T(8,128)S(1)} fusion(f32[512,256]{1,0:T(8,128)S(1)} %get-tuple-element.45, bf16[16,256]{1,0:T(8,128)(2,1)S(1)} %get-tuple-element.48, f32[16,512]{1,0:T(8,128)S(1)} %fusion.20, bf16[1,512,4096]{2,1,0:T(8,128)(2,1)} %get-tuple-element.159, bf16[1,16,4096]{2,1,0:T(8,128)(2,1)S(1)} %get-tuple-element.46), kind=kOutput, calls=%fused_computation.16 | convolution fusion | flops 71458816 | bytes 5414912 | tf_op jit(solution)/shard_map/dot_general | solution.py:30
  51.2 0.9 copy.6
  52.1 0.0 reduce-scatter.2.cloned.1.call-update
  52.1 34.5 %reduce-scatter.2.cloned.1.call-done = f32[64,256]{1,0:T(8,128)} async-done(((f32[512,256]{1,0:T(8,128)}), f32[64,256]{1,0:T(8,128)}) %reduce-scatter.2.cloned.1.call-update) | async-done | bytes 65552 | tf_op jit(solution)/shard_map/reduce_scatter | solution.py:52
  86.6 5.1 %all_gather.3 = f32[128,256]{1,0:T(8,128)S(1)} all-gather(f32[64,256]{1,0:T(8,128)} %reduce-scatter.2.cloned.1.call-done), channel_id=1, replica_groups=mesh['blk'=4,'src'=2,'layer'=4] {'src'}, dimensions={0}, use_global_device_ids=true | all-gather | bytes 196608 | tf_op jit(solution)/shard_map/all_gather | solution.py:53
  91.7 0.7 broadcast_multiply_fusion
  (14 shorter events, 0.1 us)
Async XLA Ops:
  6.5 80.0 %reduce-scatter.2.cloned.1.call-start = ((), (), s32[]{:S(2)}) async-start(), calls=%async_computation.1 | async-start | bytes 589824 | tf_op jit(solution)/shard_map/reduce_scatter | solution.py:52
  9.0 13.5 %collective-permute-start.2 = (bf16[16,256]{1,0:T(8,128)(2,1)S(1)}, bf16[16,256]{1,0:T(8,128)(2,1)S(1)}, u32[]{:S(2)}, u32[]{:S(2)}) collective-permute-start(bf16[16,256]{1,0:T(8,128)(2,1)S(1)} %copy.16), channel_id=1, source_target_pairs={{0,8},{8,16},{16,24},{24,0},{1,9},{9,17},{17,25},{25,1},{2,10},{10... | collective-permute-start | bytes 24584 | tf_op jit(solution)/shard_map/while/body/eval_jaxpr/ppermute | solution.py:11
  12.1 10.4 %collective-permute-start = (bf16[1,16,4096]{2,1,0:T(8,128)(2,1)S(1)}, bf16[1,16,4096]{2,1,0:T(8,128)(2,1)S(1)}, u32[]{:S(2)}, u32[]{:S(2)}) collective-permute-start(bf16[1,16,4096]{2,1,0:T(8,128)(2,1)S(1)} %copy.14), channel_id=1, source_target_pairs={{0,8},{8,16},{16,24},{24,0},{1,9},{9,17},{17,25},{25,1},{2,10},{10... | collective-permute-start | bytes 393224 | tf_op jit(solution)/shard_map/while/body/eval_jaxpr/ppermute | solution.py:11
  13.7 8.8 %collective-permute-start.1 = (bf16[1,16,4096]{2,1,0:T(8,128)(2,1)S(1)}, bf16[1,16,4096]{2,1,0:T(8,128)(2,1)S(1)}, u32[]{:S(2)}, u32[]{:S(2)}) collective-permute-start(bf16[1,16,4096]{2,1,0:T(8,128)(2,1)S(1)} %copy.15), channel_id=1, source_target_pairs={{0,8},{8,16},{16,24},{24,0},{1,9},{9,17},{17,25},{25,1},{2,10},{10... | collective-permute-start | bytes 393224 | tf_op jit(solution)/shard_map/while/body/eval_jaxpr/ppermute | solution.py:11
  22.6 10.7 %collective-permute-start.2 = (bf16[16,256]{1,0:T(8,128)(2,1)S(1)}, bf16[16,256]{1,0:T(8,128)(2,1)S(1)}, u32[]{:S(2)}, u32[]{:S(2)}) collective-permute-start(bf16[16,256]{1,0:T(8,128)(2,1)S(1)} %copy.16), channel_id=1, source_target_pairs={{0,8},{8,16},{16,24},{24,0},{1,9},{9,17},{17,25},{25,1},{2,10},{10... | collective-permute-start | bytes 24584 | tf_op jit(solution)/shard_map/while/body/eval_jaxpr/ppermute | solution.py:11
  22.7 10.7 %collective-permute-start = (bf16[1,16,4096]{2,1,0:T(8,128)(2,1)S(1)}, bf16[1,16,4096]{2,1,0:T(8,128)(2,1)S(1)}, u32[]{:S(2)}, u32[]{:S(2)}) collective-permute-start(bf16[1,16,4096]{2,1,0:T(8,128)(2,1)S(1)} %copy.14), channel_id=1, source_target_pairs={{0,8},{8,16},{16,24},{24,0},{1,9},{9,17},{17,25},{25,1},{2,10},{10... | collective-permute-start | bytes 393224 | tf_op jit(solution)/shard_map/while/body/eval_jaxpr/ppermute | solution.py:11
  24.5 8.8 %collective-permute-start.1 = (bf16[1,16,4096]{2,1,0:T(8,128)(2,1)S(1)}, bf16[1,16,4096]{2,1,0:T(8,128)(2,1)S(1)}, u32[]{:S(2)}, u32[]{:S(2)}) collective-permute-start(bf16[1,16,4096]{2,1,0:T(8,128)(2,1)S(1)} %copy.15), channel_id=1, source_target_pairs={{0,8},{8,16},{16,24},{24,0},{1,9},{9,17},{17,25},{25,1},{2,10},{10... | collective-permute-start | bytes 393224 | tf_op jit(solution)/shard_map/while/body/eval_jaxpr/ppermute | solution.py:11
  33.4 10.7 %collective-permute-start.2 = (bf16[16,256]{1,0:T(8,128)(2,1)S(1)}, bf16[16,256]{1,0:T(8,128)(2,1)S(1)}, u32[]{:S(2)}, u32[]{:S(2)}) collective-permute-start(bf16[16,256]{1,0:T(8,128)(2,1)S(1)} %copy.16), channel_id=1, source_target_pairs={{0,8},{8,16},{16,24},{24,0},{1,9},{9,17},{17,25},{25,1},{2,10},{10... | collective-permute-start | bytes 24584 | tf_op jit(solution)/shard_map/while/body/eval_jaxpr/ppermute | solution.py:11
  35.0 9.1 %collective-permute-start = (bf16[1,16,4096]{2,1,0:T(8,128)(2,1)S(1)}, bf16[1,16,4096]{2,1,0:T(8,128)(2,1)S(1)}, u32[]{:S(2)}, u32[]{:S(2)}) collective-permute-start(bf16[1,16,4096]{2,1,0:T(8,128)(2,1)S(1)} %copy.14), channel_id=1, source_target_pairs={{0,8},{8,16},{16,24},{24,0},{1,9},{9,17},{17,25},{25,1},{2,10},{10... | collective-permute-start | bytes 393224 | tf_op jit(solution)/shard_map/while/body/eval_jaxpr/ppermute | solution.py:11
  35.1 9.0 %collective-permute-start.1 = (bf16[1,16,4096]{2,1,0:T(8,128)(2,1)S(1)}, bf16[1,16,4096]{2,1,0:T(8,128)(2,1)S(1)}, u32[]{:S(2)}, u32[]{:S(2)}) collective-permute-start(bf16[1,16,4096]{2,1,0:T(8,128)(2,1)S(1)} %copy.15), channel_id=1, source_target_pairs={{0,8},{8,16},{16,24},{24,0},{1,9},{9,17},{17,25},{25,1},{2,10},{10... | collective-permute-start | bytes 393224 | tf_op jit(solution)/shard_map/while/body/eval_jaxpr/ppermute | solution.py:11
Sparse Core Ops, SparseCore 0:
  52.2 34.3 reduce-scatter.1
where the time goes:
time: 99.7 us; the launch traced here: 99.2 us
  waiting for transfers between devices  34.5 us (35%)
  matrix products  28.5 us (29%)
  starting transfers between devices  13.4 us (13%)
  between operations  13.4 us (13%)
  blocking collectives  5.14 us (5%)
  local copies, waits for them, and re-layouts  3.42 us (3%)
    reduce_scatter x1, waiting for transfers between devices, on_device(): lax.psum_scatter(reordered, ('src', 'layer'), scatter_dimension=0, tiled=...  34.5 us
    dot_general x4, matrix products, accumulate(): lax.dot_general(kernel, probe_rows, (((0,), (0,)), ((), ())), preferred_e...  15 us
    dot_general x4, matrix products, contract_rows(): lax.dot_general(left, right, (((1,), (1,)), ((), ())), preferred_element_...  13.5 us
    ppermute x9, starting transfers between devices, shifted(): lax.ppermute(shard, axis, [(i, (i + by) % length) for i in range(length)])  13.4 us
    all_gather x1, blocking collectives, on_device(): result = lax.all_gather(partial_rows, 'src', axis=0, tiled=True)  5.14 us
    unnamed x3, local copies, waits for them, and re-layouts  2.51 us
  transfers between devices with their start and end apart: 10, of which 1 were waited for; matrix products, arithmetic and copies ran while one was open for 22% of the time, Pallas kernels for 0%

commit v1 on v0

v1 whole, which is shorter than its diff:
```python
import functools

import jax
import jax.numpy as jnp
from jax import lax
from jax.experimental import pallas as pl
from jax.experimental.pallas import tpu as pltpu
from jax.sharding import PartitionSpec as P

MESH = pl.DeviceIdType.MESH


def kernel_body(
    n, groups, layers, chunks, inverse_width, scale,
    res_a, res_g, src_a, src_g, probes, out,
    res_v, src_v, probe_v, kern_v, kall,
    res_sem, own_sem, recv_sem, up_sem, down_sem,
    probe_sem, line_sem, relay_sem, kern_sem, kern_send,
):
    b = lax.axis_index("blk")
    s = lax.axis_index("src")
    l = lax.axis_index("layer")
    plane = groups * layers
    me = s * layers + l
    up = lax.rem(b + 1, n)
    down = lax.rem(b + n - 1, n)
    width = res_v.shape[2]
    step = width // chunks
    residents = (res_a, res_g)
    sources = (src_a, src_g)

    def peer(d):
        other = lax.rem(me + d, plane)
        return other, (b, other // layers, lax.rem(other, layers))

    def cols(c):
        return pl.ds(c * step, step)

    def resident_copy(a, c):
        return pltpu.make_async_copy(
            residents[a].at[0, :, cols(c)], res_v.at[a, :, cols(c)], res_sem.at[a, c]
        )

    def own_copy(a):
        return pltpu.make_async_copy(sources[a].at[0], src_v.at[a, b], own_sem.at[a])

    def move(source, a, c, block, going_up):
        return pltpu.make_async_remote_copy(
            src_ref=source,
            dst_ref=src_v.at[a, block, :, cols(c)],
            send_sem=(up_sem if going_up else down_sem).at[a, c, block],
            recv_sem=recv_sem.at[a, c, block],
            device_id=(up if going_up else down, s, l),
            device_id_type=MESH,
        )

    def forward(a, c, block, going_up):
        return move(src_v.at[a, block, :, cols(c)], a, c, block, going_up)

    def line_probe(e):
        return pltpu.make_async_remote_copy(
            src_ref=probes,
            dst_ref=probe_v.at[s, b],
            send_sem=line_sem.at[e],
            recv_sem=probe_sem.at[s, b],
            device_id=(lax.rem(b + e, n), s, l),
            device_id_type=MESH,
        )

    def own_probe():
        return pltpu.make_async_copy(probes, probe_v.at[s, b], probe_sem.at[s, b])

    def relay_probe(group, block, d):
        _, device = peer(d)
        return pltpu.make_async_remote_copy(
            src_ref=probe_v.at[group, block],
            dst_ref=probe_v.at[group, block],
            send_sem=relay_sem.at[block, d],
            recv_sem=probe_sem.at[group, block],
            device_id=device,
            device_id_type=MESH,
        )

    def kernel_slice(d):
        _, device = peer(d)
        return pltpu.make_async_remote_copy(
            src_ref=kern_v.at[device[2]],
            dst_ref=kall.at[l, s],
            send_sem=kern_send.at[d],
            recv_sem=kern_sem.at[me],
            device_id=device,
            device_id_type=MESH,
        )

    def kernel_arrival(d):
        other = lax.rem(me + d, plane)
        from_group, from_layer = other // layers, lax.rem(other, layers)
        return pltpu.make_async_remote_copy(
            src_ref=kern_v.at[0],
            dst_ref=kall.at[from_layer, from_group],
            send_sem=kern_send.at[d],
            recv_sem=kern_sem.at[other],
            device_id=(b, from_group, from_layer),
            device_id_type=MESH,
        )

    barrier = pltpu.get_barrier_semaphore()
    for d in range(1, plane):
        pl.semaphore_signal(barrier, inc=1, device_id=peer(d)[1], device_id_type=MESH)

    def greet(e, _):
        pl.semaphore_signal(
            barrier, inc=1, device_id=(lax.rem(b + e, n), s, l), device_id_type=MESH
        )
        return 0

    lax.fori_loop(1, n, greet, 0)
    for a in range(2):
        own_copy(a).start()
    for a in range(2):
        for c in range(chunks):
            resident_copy(a, c).start()
    pl.semaphore_wait(barrier, plane - 1 + n - 1)

    carries = lax.rem(b, layers) == l

    @pl.when(carries)
    def _():
        own_probe().start()

        def send(e, _):
            line_probe(e).start()
            return 0

        lax.fori_loop(1, n, send, 0)

    for a in range(2):
        for c in range(chunks):

            @pl.when(b < n - 1)
            def _():
                move(sources[a].at[0, :, cols(c)], a, c, b, True).start()

            @pl.when(b > 0)
            def _():
                move(sources[a].at[0, :, cols(c)], a, c, b, False).start()

    def forwarding(turn, _):
        low = b - 1 - turn
        high = b + 1 + turn
        for a in range(2):
            for c in range(chunks):

                @pl.when(low >= 0)
                def _():
                    forward(a, c, low, True).wait_recv()

                @pl.when(jnp.logical_and(low >= 0, b < n - 1))
                def _():
                    forward(a, c, low, True).start()

                @pl.when(high < n)
                def _():
                    forward(a, c, high, False).wait_recv()

                @pl.when(jnp.logical_and(high < n, b > 0))
                def _():
                    forward(a, c, high, False).start()

        return 0

    lax.fori_loop(0, n - 2, forwarding, 0)

    def relay(block, _):
        @pl.when(lax.rem(block, layers) == l)
        def _():
            relay_probe(s, block, 1).wait_recv()
            for d in range(1, plane):
                relay_probe(s, block, d).start()

        return 0

    lax.fori_loop(0, n, relay, 0)
    for a in range(2):
        own_copy(a).wait()

    grams = []
    for a in range(2):
        gram = None
        for c in range(chunks):

            @pl.when(b == 0)
            def _():
                forward(a, c, n - 1, False).wait_recv()

            @pl.when(b == n - 1)
            def _():
                forward(a, c, 0, True).wait_recv()

            resident_copy(a, c).wait()
            block = src_v[a, :, :, c * step:(c + 1) * step]
            part = lax.dot_general(
                block.reshape(block.shape[0] * block.shape[1], step),
                res_v[a, :, c * step:(c + 1) * step],
                (((1,), (1,)), ((), ())),
                preferred_element_type=jnp.float32,
            )
            gram = part if gram is None else gram + part
        grams.append(gram)
    kernel = (grams[0] * grams[1] * jnp.float32(inverse_width)).astype(jnp.bfloat16)
    share = kernel.shape[1] // layers
    for q in range(layers):
        kern_v[q] = kernel[:, q * share:(q + 1) * share]
    for d in range(1, plane):
        kernel_slice(d).start()
    kall[l, s] = kern_v[l]

    def arrived(i, _):
        group, block = i // n, lax.rem(i, n)

        @pl.when(jnp.logical_or(group != s, lax.rem(block, layers) != l))
        def _():
            relay_probe(group, block, 1).wait_recv()

        return 0

    lax.fori_loop(0, groups * n, arrived, 0)
    for d in range(1, plane):
        kernel_arrival(d).wait_recv()
    vectors = probe_v[...].reshape(groups * n * probe_v.shape[2], probe_v.shape[3])
    total = None
    for q in range(layers):
        part = lax.dot_general(
            kall[q].reshape(vectors.shape[0], share),
            vectors,
            (((0,), (0,)), ((), ())),
            preferred_element_type=jnp.float32,
        )
        total = part if total is None else total + part
    out[...] = total * jnp.float32(scale)

    for d in range(1, plane):
        kernel_slice(d).wait_send()

    def sent(block, _):
        @pl.when(jnp.logical_and(block <= b, b < n - 1))
        def _():
            for a in range(2):
                for c in range(chunks):
                    forward(a, c, block, True).wait_send()

        @pl.when(jnp.logical_and(block >= b, b > 0))
        def _():
            for a in range(2):
                for c in range(chunks):
                    forward(a, c, block, False).wait_send()

        @pl.when(lax.rem(block, layers) == l)
        def _():
            for d in range(1, plane):
                relay_probe(s, block, d).wait_send()

        @pl.when(jnp.logical_and(carries, block > 0))
        def _():
            line_probe(block).wait_send()

        return 0

    lax.fori_loop(0, n, sent, 0)


def on_device(resident_act, resident_grad, source_act, source_grad, probes):
    n = lax.axis_size("blk")
    groups = lax.axis_size("src")
    layers = lax.axis_size("layer")
    _, rows, width = resident_act.shape
    per = source_act.shape[1]
    columns = probes.shape[1]
    source_total = per * n * groups
    total_layers = resident_act.shape[0] * layers
    share = rows // layers
    plane = groups * layers
    chunks = max(1, min(4, 16 // n))
    body = functools.partial(
        kernel_body, n, groups, layers, chunks, 1.0 / width,
        (total_layers * source_total) ** (-0.5),
    )
    dma = pltpu.SemaphoreType.DMA
    return pl.pallas_call(
        body,
        out_shape=jax.ShapeDtypeStruct((share, columns), jnp.float32),
        in_specs=[pl.BlockSpec(memory_space=pl.ANY)] * 5,
        out_specs=pl.BlockSpec(memory_space=pltpu.VMEM),
        scratch_shapes=[
            pltpu.VMEM((2, rows, width), jnp.bfloat16),
            pltpu.VMEM((2, n, per, width), jnp.bfloat16),
            pltpu.VMEM((groups, n, per, columns), jnp.bfloat16),
            pltpu.VMEM((layers, n * per, share), jnp.bfloat16),
            pltpu.VMEM((layers, groups, n * per, share), jnp.bfloat16),
            dma((2, chunks)),
            dma((2,)),
            dma((2, chunks, n)),
            dma((2, chunks, n)),
            dma((2, chunks, n)),
            dma((groups, n)),
            dma((n,)),
            dma((n, plane)),
            dma((plane,)),
            dma((plane,)),
        ],
        compiler_params=pltpu.CompilerParams(
            collective_id=0, has_side_effects=True, vmem_limit_bytes=56 * 1024 * 1024
        ),
        cost_estimate=pl.CostEstimate(
            flops=4 * n * per * rows * width,
            bytes_accessed=4 * rows * width,
            transcendentals=0,
        ),
        name="ntk_product",
    )(resident_act, resident_grad, source_act, source_grad, probes)


def solution(mesh):
    in_specs = (
        P("layer", "blk", None),
        P("layer", "blk", None),
        P("layer", ("blk", "src"), None),
        P("layer", ("blk", "src"), None),
        P(("blk", "src"), None),
    )
    out_specs = P(("blk", "layer"), None)
    return jax.shard_map(
        on_device, mesh=mesh, in_specs=in_specs, out_specs=out_specs, check_vma=False
    )
```

time: 99.7 us -> 32.5 us (0.33)
  waiting for transfers between devices: 34.5 us -> 0 us
  Pallas kernels: 0 us -> 30.8 us
  matrix products: 28.5 us -> 0 us
  starting transfers between devices: 13.4 us -> 0 us
  between operations: 13.4 us -> 0.01 us
  blocking collectives: 5.14 us -> 0 us
  local copies, waits for them, and re-layouts: 3.42 us -> 1.57 us
    reduce_scatter x1 -> x0, waiting for transfers between devices: 34.5 us -> none  [on_device(): lax.psum_scatter(reordered, ('src', 'layer'), scatter_dimension=0, tiled=...]
    pallas_call x0 -> x1, Pallas kernels: none -> 30.8 us  [on_device(): pl.pallas_call(body, out_shape=jax.ShapeDtypeStruct((share, columns), jnp...]
    dot_general x8 -> x0, matrix products: 28.5 us -> none  [the longest x4 15 us: accumulate(): lax.dot_general(kernel, probe_rows, (((0,), (0,)), ((), ())), preferred_e...]
    ppermute x9 -> x0, starting transfers between devices: 13.4 us -> none  [shifted(): lax.ppermute(shard, axis, [(i, (i + by) % length) for i in range(length)])]
    all_gather x1 -> x0, blocking collectives: 5.14 us -> none  [on_device(): result = lax.all_gather(partial_rows, 'src', axis=0, tiled=True)]
    unnamed x3 -> x1, local copies, waits for them, and re-layouts: 2.51 us -> 1.57 us
  transfers between devices with their start and end apart: 10 -> 0, of which waited for: 1 -> 0; matrix products, arithmetic and copies ran while one was open for 22% -> 0% of each run, Pallas kernels for 0% -> 0%
where the time goes in v1:
time: 32.5 us; the launch traced here: 32.3 us
  Pallas kernels  30.8 us (95%)
  local copies, waits for them, and re-layouts  1.57 us (5%)
    pallas_call x1, Pallas kernels, on_device(): pl.pallas_call(body, out_shape=jax.ShapeDtypeStruct((share, columns), jnp...  30.8 us
    unnamed x1, local copies, waits for them, and re-layouts  1.57 us

profile of v1, /device:TPU:0, one launch (start us, length us, event | category | flops | bytes accessed | tf_op | source)
XLA Modules:
  0.0 32.3 jit_solution(8140787840787410933)
XLA Ops:
  0.0 30.8 %ntk_product.1 = f32[128,256]{1,0:T(8,128)} custom-call(bf16[1,512,4096]{2,1,0:T(8,128)(2,1)} %res_a.1, bf16[1,512,4096]{2,1,0:T(8,128)(2,1)} %res_g.1, bf16[1,16,4096]{2,1,0:T(8,128)(2,1)} %src_a.1, bf16[1,16,4096]{2,1,0:T(8,128)(2,1)} %src_g.1, bf16[16,256]{1,0:T(8,128)(2,1)} %probes.1), custom_call_target="tpu_custom_call" | custom-call | flops 536870912 | bytes 8388608 | tf_op jit(solution)/shard_map/ntk_product/pallas_call | solution.py:289
  30.8 1.6 %copy.7 = f32[128,256]{1,0:T(8,128)} copy(f32[128,256]{1,0:T(8,128)} %ntk_product.1) | data formatting | bytes 262144

commit v2 on v1

v2 whole, which is shorter than its diff:
```python
import functools

import jax
import jax.numpy as jnp
from jax import lax
from jax.experimental import pallas as pl
from jax.experimental.pallas import tpu as pltpu
from jax.sharding import PartitionSpec as P

MESH = pl.DeviceIdType.MESH


def kernel_body(
    n, groups, layers, chunks, flight, inverse_width, scale,
    res_a, res_g, src_a, src_g, probes, out,
    res_v, src_v, probe_v, near_v, far_v, near_all, far_all,
    res_sem, own_sem, recv_sem, up_sem, down_sem,
    probe_sem, line_up, line_down, relay_sem,
    near_sem, near_send, far_sem, far_send,
):
    b = lax.axis_index("blk")
    s = lax.axis_index("src")
    l = lax.axis_index("layer")
    plane = groups * layers
    me = s * layers + l
    up = lax.rem(b + 1, n)
    down = lax.rem(b + n - 1, n)
    width = res_v.shape[2]
    step = width // chunks
    residents = (res_a, res_g)
    sources = (src_a, src_g)
    items = [(a, c) for a in range(2) for c in range(chunks)]
    has_up = b < n - 1
    has_down = b > 0

    def slot(position, block):
        return jnp.where(2 * position < n, block, n - 1 - block)

    def device_of(other):
        return (b, other // layers, lax.rem(other, layers))

    def peer(d):
        return device_of(lax.rem(me + d, plane))

    def cols(c):
        return pl.ds(c * step, step)

    def resident_copy(a, c):
        return pltpu.make_async_copy(
            residents[a].at[0, :, cols(c)], res_v.at[a, :, cols(c)], res_sem.at[a, c]
        )

    def own_copy(a):
        return pltpu.make_async_copy(
            sources[a].at[0], src_v.at[a, slot(b, b)], own_sem.at[a]
        )

    def move(source, a, c, block, going_up):
        to = up if going_up else down
        return pltpu.make_async_remote_copy(
            src_ref=source,
            dst_ref=src_v.at[a, slot(to, block), :, cols(c)],
            send_sem=(up_sem if going_up else down_sem).at[a, c, block],
            recv_sem=recv_sem.at[a, c, block],
            device_id=(to, s, l),
            device_id_type=MESH,
        )

    def own(a, c, going_up):
        return move(sources[a].at[0, :, cols(c)], a, c, b, going_up)

    def forward(a, c, block, going_up):
        return move(src_v.at[a, slot(b, block), :, cols(c)], a, c, block, going_up)

    def arrive(a, c, block):
        here = src_v.at[a, slot(b, block), :, cols(c)]
        return pltpu.make_async_copy(here, here, recv_sem.at[a, c, block])

    def line_probe(block, going_up, source=None):
        to = up if going_up else down
        return pltpu.make_async_remote_copy(
            src_ref=probe_v.at[s, slot(b, block)] if source is None else source,
            dst_ref=probe_v.at[s, slot(to, block)],
            send_sem=(line_up if going_up else line_down).at[block],
            recv_sem=probe_sem.at[s, block],
            device_id=(to, s, l),
            device_id_type=MESH,
        )

    def own_probe():
        return pltpu.make_async_copy(
            probes, probe_v.at[s, slot(b, b)], probe_sem.at[s, b]
        )

    def probe_arrive(group, block):
        here = probe_v.at[group, slot(b, block)]
        return pltpu.make_async_copy(here, here, probe_sem.at[group, block])

    def relay_probe(block, d):
        here = probe_v.at[s, slot(b, block)]
        return pltpu.make_async_remote_copy(
            src_ref=here,
            dst_ref=here,
            send_sem=relay_sem.at[block, d],
            recv_sem=probe_sem.at[s, block],
            device_id=peer(d),
            device_id_type=MESH,
        )

    def kernel_slice(d, far):
        device = peer(d)
        return pltpu.make_async_remote_copy(
            src_ref=(far_v if far else near_v).at[device[2]],
            dst_ref=(far_all if far else near_all).at[l, s],
            send_sem=(far_send if far else near_send).at[d],
            recv_sem=(far_sem if far else near_sem).at[me],
            device_id=device,
            device_id_type=MESH,
        )

    def kernel_arrive(d, far):
        other = lax.rem(me + d, plane)
        _, from_group, from_layer = device_of(other)
        here = (far_all if far else near_all).at[from_layer, from_group]
        return pltpu.make_async_copy(here, here, (far_sem if far else near_sem).at[other])

    def signal(device):
        pl.semaphore_signal(
            pltpu.get_barrier_semaphore(), inc=1, device_id=device, device_id_type=MESH
        )

    @pl.when(has_down)
    def _():
        signal((down, s, l))

    @pl.when(has_up)
    def _():
        signal((up, s, l))

    for d in range(1, plane):
        signal(peer(d))
    carries = lax.rem(b, layers) == l

    @pl.when(carries)
    def _():
        own_probe().start()

    for a in range(2):
        own_copy(a).start()
    for a, c in items:
        resident_copy(a, c).start()
    pl.semaphore_wait(
        pltpu.get_barrier_semaphore(),
        plane - 1 + has_up.astype(jnp.int32) + has_down.astype(jnp.int32),
    )

    @pl.when(jnp.logical_and(carries, has_down))
    def _():
        line_probe(b, False, probes).start()

    @pl.when(jnp.logical_and(carries, has_up))
    def _():
        line_probe(b, True, probes).start()

    for k, (a, c) in enumerate(items):
        for going_up, has in ((False, has_down), (True, has_up)):

            @pl.when(has)
            def _():
                if k >= flight:
                    forward(*items[k - flight], b, going_up).wait_send()
                own(a, c, going_up).start()

    def forwarding(turn, _):
        low = b - 1 - turn
        high = b + 1 + turn
        for block, inside, going_up, has in (
            (high, high < n, False, has_down),
            (low, low >= 0, True, has_up),
        ):
            probe_here = jnp.logical_and(inside, lax.rem(jnp.maximum(block, 0), layers) == l)

            @pl.when(probe_here)
            def _():
                probe_arrive(s, block).wait()

            @pl.when(jnp.logical_and(probe_here, has))
            def _():
                line_probe(block, going_up).start()

        for k, (a, c) in enumerate(items):
            for block, inside, going_up, has in (
                (high, high < n, False, has_down),
                (low, low >= 0, True, has_up),
            ):
                before = items[k - flight]
                earlier = block if k >= flight else (block + 1 if going_up else block - 1)

                @pl.when(inside)
                def _():
                    arrive(a, c, block).wait()

                @pl.when(jnp.logical_and(inside, has))
                def _():
                    forward(*before, earlier, going_up).wait_send()
                    forward(a, c, block, going_up).start()

        return 0

    lax.fori_loop(0, n - 2, forwarding, 0)
    for a in range(2):
        own_copy(a).wait()

    def product(grams, buffer):
        kernel = (grams[0] * grams[1] * jnp.float32(inverse_width)).astype(jnp.bfloat16)
        share = kernel.shape[1] // layers
        for q in range(layers):
            buffer[q] = kernel[:, q * share:(q + 1) * share]

    def gram(a, far):
        total = None
        for c in range(chunks):
            if far:

                @pl.when(b == 0)
                def _():
                    arrive(a, c, n - 1).wait()

                @pl.when(b == n - 1)
                def _():
                    arrive(a, c, 0).wait()

                block = src_v[a, n - 1, :, c * step:(c + 1) * step]
            else:
                resident_copy(a, c).wait()
                block = src_v[a, 0:n - 1, :, c * step:(c + 1) * step]
                block = block.reshape(block.shape[0] * block.shape[1], step)
            part = lax.dot_general(
                block,
                res_v[a, :, c * step:(c + 1) * step],
                (((1,), (1,)), ((), ())),
                preferred_element_type=jnp.float32,
            )
            total = part if total is None else total + part
        return total

    product([gram(a, False) for a in range(2)], near_v)
    for d in range(1, plane):
        kernel_slice(d, False).start()
    near_all[l, s] = near_v[l]

    def relay(block, _):
        @pl.when(lax.rem(block, layers) == l)
        def _():
            at_end = jnp.logical_or(
                jnp.logical_and(b == 0, block == n - 1),
                jnp.logical_and(b == n - 1, block == 0),
            )

            @pl.when(jnp.logical_or(block == b, at_end))
            def _():
                probe_arrive(s, block).wait()

            for d in range(1, plane):
                relay_probe(block, d).start()

        return 0

    lax.fori_loop(0, n, relay, 0)

    product([gram(a, True) for a in range(2)], far_v)
    for d in range(1, plane):
        kernel_slice(d, True).start()
    far_all[l, s] = far_v[l]

    def arrived(i, _):
        group, block = i // n, lax.rem(i, n)

        @pl.when(jnp.logical_or(group != s, lax.rem(block, layers) != l))
        def _():
            probe_arrive(group, block).wait()

        return 0

    lax.fori_loop(0, groups * n, arrived, 0)

    def contract(everything, vectors):
        depth, columns = vectors.shape[0] * vectors.shape[1], vectors.shape[2]
        total = None
        for q in range(layers):
            part = lax.dot_general(
                everything[q].reshape(depth, everything.shape[3]),
                vectors.reshape(depth, columns),
                (((0,), (0,)), ((), ())),
                preferred_element_type=jnp.float32,
            )
            total = part if total is None else total + part
        return total

    for d in range(1, plane):
        kernel_arrive(d, False).wait()
    near_vectors = probe_v[:, 0:n - 1]
    near = contract(
        near_all,
        near_vectors.reshape(groups, (n - 1) * probe_v.shape[2], probe_v.shape[3]),
    )

    def sent(block, _):
        @pl.when(lax.rem(block, layers) == l)
        def _():
            for d in range(1, plane):
                relay_probe(block, d).wait_send()

            @pl.when(jnp.logical_and(has_up, block <= b))
            def _():
                line_probe(block, True).wait_send()

            @pl.when(jnp.logical_and(has_down, block >= b))
            def _():
                line_probe(block, False).wait_send()

        return 0

    lax.fori_loop(0, n, sent, 0)
    for block, going_up, has in ((n - 1, False, has_down), (0, True, has_up)):

        @pl.when(has)
        def _():
            for a, c in items[-flight:]:
                forward(a, c, block, going_up).wait_send()

    for d in range(1, plane):
        kernel_slice(d, False).wait_send()
    for d in range(1, plane):
        kernel_arrive(d, True).wait()
    out[...] = (near + contract(far_all, probe_v[:, n - 1])) * jnp.float32(scale)
    for d in range(1, plane):
        kernel_slice(d, True).wait_send()


def on_device(resident_act, resident_grad, source_act, source_grad, probes):
    n = lax.axis_size("blk")
    groups = lax.axis_size("src")
    layers = lax.axis_size("layer")
    _, rows, width = resident_act.shape
    per = source_act.shape[1]
    columns = probes.shape[1]
    source_total = per * n * groups
    total_layers = resident_act.shape[0] * layers
    share = rows // layers
    plane = groups * layers
    chunks = max(1, min(4, 16 // n))
    flight = min(3, 2 * chunks)
    body = functools.partial(
        kernel_body, n, groups, layers, chunks, flight, 1.0 / width,
        (total_layers * source_total) ** (-0.5),
    )
    dma = pltpu.SemaphoreType.DMA
    return pl.pallas_call(
        body,
        out_shape=jax.ShapeDtypeStruct((share, columns), jnp.float32),
        in_specs=[pl.BlockSpec(memory_space=pl.ANY)] * 5,
        out_specs=pl.BlockSpec(memory_space=pltpu.VMEM),
        scratch_shapes=[
            pltpu.VMEM((2, rows, width), jnp.bfloat16),
            pltpu.VMEM((2, n, per, width), jnp.bfloat16),
            pltpu.VMEM((groups, n, per, columns), jnp.bfloat16),
            pltpu.VMEM((layers, (n - 1) * per, share), jnp.bfloat16),
            pltpu.VMEM((layers, per, share), jnp.bfloat16),
            pltpu.VMEM((layers, groups, (n - 1) * per, share), jnp.bfloat16),
            pltpu.VMEM((layers, groups, per, share), jnp.bfloat16),
            dma((2, chunks)),
            dma((2,)),
            dma((2, chunks, n)),
            dma((2, chunks, n)),
            dma((2, chunks, n)),
            dma((groups, n)),
            dma((n,)),
            dma((n,)),
            dma((n, plane)),
            dma((plane,)),
            dma((plane,)),
            dma((plane,)),
            dma((plane,)),
        ],
        compiler_params=pltpu.CompilerParams(
            collective_id=0, has_side_effects=True, vmem_limit_bytes=56 * 1024 * 1024
        ),
        cost_estimate=pl.CostEstimate(
            flops=4 * n * per * rows * width,
            bytes_accessed=4 * rows * width,
            transcendentals=0,
        ),
        name="ntk_product",
    )(resident_act, resident_grad, source_act, source_grad, probes)


def solution(mesh):
    in_specs = (
        P("layer", "blk", None),
        P("layer", "blk", None),
        P("layer", ("blk", "src"), None),
        P("layer", ("blk", "src"), None),
        P(("blk", "src"), None),
    )
    out_specs = P(("blk", "layer"), None)
    return jax.shard_map(
        on_device, mesh=mesh, in_specs=in_specs, out_specs=out_specs, check_vma=False
    )
```

time: 32.5 us -> 32.2 us (level)
  Pallas kernels: 30.8 us -> 30.1 us
    pallas_call x1, Pallas kernels: 30.8 us -> 30.1 us  [on_device(): pl.pallas_call(body, out_shape=jax.ShapeDtypeStruct((share, columns), jnp...]
where the time goes in v2:
time: 32.2 us; the launch traced here: 31.7 us
  Pallas kernels  30.1 us (93%)
  local copies, waits for them, and re-layouts  1.57 us (5%)
    pallas_call x1, Pallas kernels, on_device(): pl.pallas_call(body, out_shape=jax.ShapeDtypeStruct((share, columns), jnp...  30.1 us
    unnamed x1, local copies, waits for them, and re-layouts  1.57 us

profile of v2, /device:TPU:0, one launch (start us, length us, event | category | flops | bytes accessed | tf_op | source)
XLA Modules:
  0.0 31.7 jit_solution(413980414685856253)
XLA Ops:
  0.0 30.1 %ntk_product.1 = f32[128,256]{1,0:T(8,128)} custom-call(bf16[1,512,4096]{2,1,0:T(8,128)(2,1)} %res_a.1, bf16[1,512,4096]{2,1,0:T(8,128)(2,1)} %res_g.1, bf16[1,16,4096]{2,1,0:T(8,128)(2,1)} %src_a.1, bf16[1,16,4096]{2,1,0:T(8,128)(2,1)} %src_g.1, bf16[16,256]{1,0:T(8,128)(2,1)} %probes.1), custom_call_target="tpu_custom_call" | custom-call | flops 536870912 | bytes 8388608 | tf_op jit(solution)/shard_map/ntk_product/pallas_call | solution.py:359
  30.2 1.6 %copy.7 = f32[128,256]{1,0:T(8,128)} copy(f32[128,256]{1,0:T(8,128)} %ntk_product.1) | data formatting | bytes 262144

commit v3 on v2

--- a/solution.py
+++ b/solution.py
@@ -212,7 +212,7 @@
         own_copy(a).wait()
 
     def product(grams, buffer):
-        kernel = (grams[0] * grams[1] * jnp.float32(inverse_width)).astype(jnp.bfloat16)
+        kernel = (grams[0] * grams[1] * jnp.float32(inverse_width)).T.astype(jnp.bfloat16)
         share = kernel.shape[1] // layers
         for q in range(layers):
             buffer[q] = kernel[:, q * share:(q + 1) * share]
@@ -236,8 +236,8 @@
                 block = src_v[a, 0:n - 1, :, c * step:(c + 1) * step]
                 block = block.reshape(block.shape[0] * block.shape[1], step)
             part = lax.dot_general(
+                res_v[a, :, c * step:(c + 1) * step],
                 block,
-                res_v[a, :, c * step:(c + 1) * step],
                 (((1,), (1,)), ((), ())),
                 preferred_element_type=jnp.float32,
             )

time: 32.2 us -> 36 us (1.12)
  Pallas kernels: 30.1 us -> 34 us
    pallas_call x1, Pallas kernels: 30.1 us -> 34 us  [on_device(): pl.pallas_call(body, out_shape=jax.ShapeDtypeStruct((share, columns), jnp...]
where the time goes in v3:
time: 36 us; the launch traced here: 35.6 us
  Pallas kernels  34 us (94%)
  local copies, waits for them, and re-layouts  1.57 us (4%)
    pallas_call x1, Pallas kernels, on_device(): pl.pallas_call(body, out_shape=jax.ShapeDtypeStruct((share, columns), jnp...  34 us
    unnamed x1, local copies, waits for them, and re-layouts  1.57 us

profile of v3, /device:TPU:0, one launch (start us, length us, event | category | flops | bytes accessed | tf_op | source)
XLA Modules:
  0.0 35.6 jit_solution(8345032508078792862)
XLA Ops:
  0.0 34.0 %ntk_product.1 = f32[128,256]{1,0:T(8,128)} custom-call(bf16[1,512,4096]{2,1,0:T(8,128)(2,1)} %res_a.1, bf16[1,512,4096]{2,1,0:T(8,128)(2,1)} %res_g.1, bf16[1,16,4096]{2,1,0:T(8,128)(2,1)} %src_a.1, bf16[1,16,4096]{2,1,0:T(8,128)(2,1)} %src_g.1, bf16[16,256]{1,0:T(8,128)(2,1)} %probes.1), custom_call_target="tpu_custom_call" | custom-call | flops 536870912 | bytes 8388608 | tf_op jit(solution)/shard_map/ntk_product/pallas_call | solution.py:359
  34.0 1.6 %copy.7 = f32[128,256]{1,0:T(8,128)} copy(f32[128,256]{1,0:T(8,128)} %ntk_product.1) | data formatting | bytes 262144

commit v4 on v2

--- a/solution.py
+++ b/solution.py
@@ -207,36 +207,28 @@
 
         return 0
 
-    lax.fori_loop(0, n - 2, forwarding, 0)
+    at_end = jnp.logical_or(b == 0, b == n - 1)
+    lax.fori_loop(0, n - 3, forwarding, 0)
     for a in range(2):
         own_copy(a).wait()
 
-    def product(grams, buffer):
+    def product(grams, buffers):
         kernel = (grams[0] * grams[1] * jnp.float32(inverse_width)).astype(jnp.bfloat16)
         share = kernel.shape[1] // layers
-        for q in range(layers):
-            buffer[q] = kernel[:, q * share:(q + 1) * share]
-
-    def gram(a, far):
+        row = 0
+        for buffer in buffers:
+            rows = buffer.shape[1]
+            for q in range(layers):
+                buffer[q] = kernel[row:row + rows, q * share:(q + 1) * share]
+            row += rows
+
+    def gram(a, first, last, ready):
         total = None
         for c in range(chunks):
-            if far:
-
-                @pl.when(b == 0)
-                def _():
-                    arrive(a, c, n - 1).wait()
-
-                @pl.when(b == n - 1)
-                def _():
-                    arrive(a, c, 0).wait()
-
-                block = src_v[a, n - 1, :, c * step:(c + 1) * step]
-            else:
-                resident_copy(a, c).wait()
-                block = src_v[a, 0:n - 1, :, c * step:(c + 1) * step]
-                block = block.reshape(block.shape[0] * block.shape[1], step)
+            ready(a, c)
+            block = src_v[a, first:last, :, c * step:(c + 1) * step]
             part = lax.dot_general(
-                block,
+                block.reshape(block.shape[0] * block.shape[1], step),
                 res_v[a, :, c * step:(c + 1) * step],
                 (((1,), (1,)), ((), ())),
                 preferred_element_type=jnp.float32,
@@ -244,20 +236,30 @@
             total = part if total is None else total + part
         return total
 
-    product([gram(a, False) for a in range(2)], near_v)
-    for d in range(1, plane):
-        kernel_slice(d, False).start()
-    near_all[l, s] = near_v[l]
+    def resident_ready(a, c):
+        resident_copy(a, c).wait()
+
+    def farthest_ready(a, c):
+        for distance in (n - 2, n - 1):
+            arrive(a, c, jnp.where(b == 0, distance, n - 1 - distance)).wait()
+
+    @pl.when(at_end)
+    def _():
+        product([gram(a, 0, n - 2, resident_ready) for a in range(2)], (near_v,))
+        for d in range(1, plane):
+            kernel_slice(d, False).start()
+
+    @pl.when(jnp.logical_not(at_end))
+    def _():
+        forwarding(n - 3, 0)
 
     def relay(block, _):
         @pl.when(lax.rem(block, layers) == l)
         def _():
-            at_end = jnp.logical_or(
-                jnp.logical_and(b == 0, block == n - 1),
-                jnp.logical_and(b == n - 1, block == 0),
-            )
-
-            @pl.when(jnp.logical_or(block == b, at_end))
+            gap = jnp.abs(block - b)
+            unseen = jnp.logical_and(at_end, gap >= n - 2)
+
+            @pl.when(jnp.logical_or(block == b, unseen))
             def _():
                 probe_arrive(s, block).wait()
 
@@ -268,7 +270,17 @@
 
     lax.fori_loop(0, n, relay, 0)
 
-    product([gram(a, True) for a in range(2)], far_v)
+    @pl.when(at_end)
+    def _():
+        product([gram(a, n - 2, n, farthest_ready) for a in range(2)], (far_v,))
+
+    @pl.when(jnp.logical_not(at_end))
+    def _():
+        product([gram(a, 0, n, resident_ready) for a in range(2)], (near_v, far_v))
+        for d in range(1, plane):
+            kernel_slice(d, False).start()
+
+    near_all[l, s] = near_v[l]
     for d in range(1, plane):
         kernel_slice(d, True).start()
     far_all[l, s] = far_v[l]
@@ -299,10 +311,10 @@
 
     for d in range(1, plane):
         kernel_arrive(d, False).wait()
-    near_vectors = probe_v[:, 0:n - 1]
+    near_vectors = probe_v[:, 0:n - 2]
     near = contract(
         near_all,
-        near_vectors.reshape(groups, (n - 1) * probe_v.shape[2], probe_v.shape[3]),
+        near_vectors.reshape(groups, (n - 2) * probe_v.shape[2], probe_v.shape[3]),
     )
 
     def sent(block, _):
@@ -333,7 +345,12 @@
         kernel_slice(d, False).wait_send()
     for d in range(1, plane):
         kernel_arrive(d, True).wait()
-    out[...] = (near + contract(far_all, probe_v[:, n - 1])) * jnp.float32(scale)
+    far_vectors = probe_v[:, n - 2:n]
+    far = contract(
+        far_all,
+        far_vectors.reshape(groups, 2 * probe_v.shape[2], probe_v.shape[3]),
+    )
+    out[...] = (near + far) * jnp.float32(scale)
     for d in range(1, plane):
         kernel_slice(d, True).wait_send()
 
@@ -365,10 +382,10 @@
             pltpu.VMEM((2, rows, width), jnp.bfloat16),
             pltpu.VMEM((2, n, per, width), jnp.bfloat16),
             pltpu.VMEM((groups, n, per, columns), jnp.bfloat16),
-            pltpu.VMEM((layers, (n - 1) * per, share), jnp.bfloat16),
-            pltpu.VMEM((layers, per, share), jnp.bfloat16),
-            pltpu.VMEM((layers, groups, (n - 1) * per, share), jnp.bfloat16),
-            pltpu.VMEM((layers, groups, per, share), jnp.bfloat16),
+            pltpu.VMEM((layers, (n - 2) * per, share), jnp.bfloat16),
+            pltpu.VMEM((layers, 2 * per, share), jnp.bfloat16),
+            pltpu.VMEM((layers, groups, (n - 2) * per, share), jnp.bfloat16),
+            pltpu.VMEM((layers, groups, 2 * per, share), jnp.bfloat16),
             dma((2, chunks)),
             dma((2,)),
             dma((2, chunks, n)),

time: 32.2 us -> 31.4 us (0.975); the launches traced: 31.7 us -> 31.3 us
  Pallas kernels: 30.1 us -> 29.7 us
    pallas_call x1, Pallas kernels: 30.1 us -> 29.7 us  [on_device(): pl.pallas_call(body, out_shape=jax.ShapeDtypeStruct((share, columns), jnp...]
where the time goes in v4:
time: 31.4 us; the launch traced here: 31.3 us
  Pallas kernels  29.7 us (95%)
  local copies, waits for them, and re-layouts  1.57 us (5%)
    pallas_call x1, Pallas kernels, on_device(): pl.pallas_call(body, out_shape=jax.ShapeDtypeStruct((share, columns), jnp...  29.7 us
    unnamed x1, local copies, waits for them, and re-layouts  1.57 us

profile of v4, /device:TPU:0, one launch (start us, length us, event | category | flops | bytes accessed | tf_op | source)
XLA Modules:
  0.0 31.3 jit_solution(4168927831413580974)
XLA Ops:
  0.0 29.7 %ntk_product.1 = f32[128,256]{1,0:T(8,128)} custom-call(bf16[1,512,4096]{2,1,0:T(8,128)(2,1)} %res_a.1, bf16[1,512,4096]{2,1,0:T(8,128)(2,1)} %res_g.1, bf16[1,16,4096]{2,1,0:T(8,128)(2,1)} %src_a.1, bf16[1,16,4096]{2,1,0:T(8,128)(2,1)} %src_g.1, bf16[16,256]{1,0:T(8,128)(2,1)} %probes.1), custom_call_target="tpu_custom_call" | custom-call | flops 536870912 | bytes 8388608 | tf_op jit(solution)/shard_map/ntk_product/pallas_call | solution.py:376
  29.7 1.6 %copy.7 = f32[128,256]{1,0:T(8,128)} copy(f32[128,256]{1,0:T(8,128)} %ntk_product.1) | data formatting | bytes 262144

commit v5 on v4

--- a/solution.py
+++ b/solution.py
@@ -367,7 +367,7 @@
     share = rows // layers
     plane = groups * layers
     chunks = max(1, min(4, 16 // n))
-    flight = min(3, 2 * chunks)
+    flight = 2 * chunks
     body = functools.partial(
         kernel_body, n, groups, layers, chunks, flight, 1.0 / width,
         (total_layers * source_total) ** (-0.5),

time: 31.4 us -> 31.3 us (level)
  no operation moved by 1% of the time
where the time goes in v5:
time: 31.3 us; the launch traced here: 31.2 us
  Pallas kernels  29.6 us (95%)
  local copies, waits for them, and re-layouts  1.57 us (5%)
    pallas_call x1, Pallas kernels, on_device(): pl.pallas_call(body, out_shape=jax.ShapeDtypeStruct((share, columns), jnp...  29.6 us
    unnamed x1, local copies, waits for them, and re-layouts  1.57 us

profile of v5, /device:TPU:0, one launch (start us, length us, event | category | flops | bytes accessed | tf_op | source)
XLA Modules:
  0.0 31.2 jit_solution(15093568480728907005)
XLA Ops:
  0.0 29.6 %ntk_product.1 = f32[128,256]{1,0:T(8,128)} custom-call(bf16[1,512,4096]{2,1,0:T(8,128)(2,1)} %res_a.1, bf16[1,512,4096]{2,1,0:T(8,128)(2,1)} %res_g.1, bf16[1,16,4096]{2,1,0:T(8,128)(2,1)} %src_a.1, bf16[1,16,4096]{2,1,0:T(8,128)(2,1)} %src_g.1, bf16[16,256]{1,0:T(8,128)(2,1)} %probes.1), custom_call_target="tpu_custom_call" | custom-call | flops 536870912 | bytes 8388608 | tf_op jit(solution)/shard_map/ntk_product/pallas_call | solution.py:376
  29.6 1.6 %copy.7 = f32[128,256]{1,0:T(8,128)} copy(f32[128,256]{1,0:T(8,128)} %ntk_product.1) | data formatting | bytes 262144

commit v6 on v5

--- a/solution.py
+++ b/solution.py
@@ -350,7 +350,7 @@
         far_all,
         far_vectors.reshape(groups, 2 * probe_v.shape[2], probe_v.shape[3]),
     )
-    out[...] = (near + far) * jnp.float32(scale)
+    out[...] = near + far
     for d in range(1, plane):
         kernel_slice(d, True).wait_send()
 
@@ -367,15 +367,15 @@
     share = rows // layers
     plane = groups * layers
     chunks = max(1, min(4, 16 // n))
-    flight = 2 * chunks
+    flight = min(5, 2 * chunks)
     body = functools.partial(
         kernel_body, n, groups, layers, chunks, flight, 1.0 / width,
         (total_layers * source_total) ** (-0.5),
     )
     dma = pltpu.SemaphoreType.DMA
-    return pl.pallas_call(
+    total = pl.pallas_call(
         body,
-        out_shape=jax.ShapeDtypeStruct((share, columns), jnp.float32),
+        out_shape=pltpu.VMEM((share, columns), jnp.float32),
         in_specs=[pl.BlockSpec(memory_space=pl.ANY)] * 5,
         out_specs=pl.BlockSpec(memory_space=pltpu.VMEM),
         scratch_shapes=[
@@ -410,6 +410,7 @@
         ),
         name="ntk_product",
     )(resident_act, resident_grad, source_act, source_grad, probes)
+    return total * jnp.float32((total_layers * source_total) ** (-0.5))
 
 
 def solution(mesh):

time: 31.3 us -> 29.8 us (0.952)
  local copies, waits for them, and re-layouts: 1.57 us -> 0 us
  other arithmetic: 0 us -> 0.67 us
  Pallas kernels: 29.6 us -> 29 us
    unnamed x1 -> x0, local copies, waits for them, and re-layouts: 1.57 us -> none
    mul x0 -> x1, other arithmetic: none -> 0.67 us  [on_device(): return total * jnp.float32((total_layers * source_total) ** (-0.5))]
    pallas_call x1, Pallas kernels: 29.6 us -> 29 us  [on_device(): pl.pallas_call(body, out_shape=pltpu.VMEM((share, columns), jnp.float32),...]
where the time goes in v6:
time: 29.8 us; the launch traced here: 29.6 us
  Pallas kernels  29 us (97%)
  other arithmetic  0.67 us (2%)
    pallas_call x1, Pallas kernels, on_device(): pl.pallas_call(body, out_shape=pltpu.VMEM((share, columns), jnp.float32),...  29 us
    mul x1, other arithmetic, on_device(): return total * jnp.float32((total_layers * source_total) ** (-0.5))  0.67 us

profile of v6, /device:TPU:0, one launch (start us, length us, event | category | flops | bytes accessed | tf_op | source)
XLA Modules:
  0.0 29.6 jit_solution(5221454701642301292)
XLA Ops:
  0.0 29.0 %ntk_product.1 = f32[128,256]{1,0:T(8,128)S(1)} custom-call(bf16[1,512,4096]{2,1,0:T(8,128)(2,1)} %res_a.1, bf16[1,512,4096]{2,1,0:T(8,128)(2,1)} %res_g.1, bf16[1,16,4096]{2,1,0:T(8,128)(2,1)} %src_a.1, bf16[1,16,4096]{2,1,0:T(8,128)(2,1)} %src_g.1, bf16[16,256]{1,0:T(8,128)(2,1)} %probes.1), custom_call_target="tpu_custom_call" | custom-call | flops 536870912 | bytes 8388608 | tf_op jit(solution)/shard_map/ntk_product/pallas_call | solution.py:376
  29.0 0.7 %broadcast_multiply_fusion = f32[128,256]{1,0:T(8,128)} fusion(f32[128,256]{1,0:T(8,128)S(1)} %ntk_product.1), kind=kLoop, calls=%fused_computation | loop fusion | flops 32768 | bytes 262144 | tf_op jit(solution)/shard_map/mul | solution.py:413

commit v7 on v6

--- a/solution.py
+++ b/solution.py
@@ -366,8 +366,8 @@
     total_layers = resident_act.shape[0] * layers
     share = rows // layers
     plane = groups * layers
-    chunks = max(1, min(4, 16 // n))
-    flight = min(5, 2 * chunks)
+    chunks = max(1, min(2, 16 // n))
+    flight = min(3, 2 * chunks)
     body = functools.partial(
         kernel_body, n, groups, layers, chunks, flight, 1.0 / width,
         (total_layers * source_total) ** (-0.5),

time: 29.8 us -> 30 us (level)
  no operation moved by 1% of the time
where the time goes in v7:
time: 30 us; the launch traced here: 29.8 us
  Pallas kernels  29.2 us (97%)
  other arithmetic  0.67 us (2%)
    pallas_call x1, Pallas kernels, on_device(): pl.pallas_call(body, out_shape=pltpu.VMEM((share, columns), jnp.float32),...  29.2 us
    mul x1, other arithmetic, on_device(): return total * jnp.float32((total_layers * source_total) ** (-0.5))  0.67 us

profile of v7, /device:TPU:0, one launch (start us, length us, event | category | flops | bytes accessed | tf_op | source)
XLA Modules:
  0.0 29.8 jit_solution(16430244984643953762)
XLA Ops:
  0.0 29.2 %ntk_product.1 = f32[128,256]{1,0:T(8,128)S(1)} custom-call(bf16[1,512,4096]{2,1,0:T(8,128)(2,1)} %res_a.1, bf16[1,512,4096]{2,1,0:T(8,128)(2,1)} %res_g.1, bf16[1,16,4096]{2,1,0:T(8,128)(2,1)} %src_a.1, bf16[1,16,4096]{2,1,0:T(8,128)(2,1)} %src_g.1, bf16[16,256]{1,0:T(8,128)(2,1)} %probes.1), custom_call_target="tpu_custom_call" | custom-call | flops 536870912 | bytes 8388608 | tf_op jit(solution)/shard_map/ntk_product/pallas_call | solution.py:376
  29.2 0.7 %broadcast_multiply_fusion = f32[128,256]{1,0:T(8,128)} fusion(f32[128,256]{1,0:T(8,128)S(1)} %ntk_product.1), kind=kLoop, calls=%fused_computation | loop fusion | flops 32768 | bytes 262144 | tf_op jit(solution)/shard_map/mul | solution.py:413
